TPU v7x, 128 devices: a whole 4x4x4 slice. The times are simulated.
128 devices in a mesh: item: 16 (over z, y), code: 8 (over x, core).
Axes of the slice: x: 4, y: 4, z: 4, core: 2. Of those that a mesh axis runs over, the one named last changes fastest.
Arguments:
- residuals: float32 [256, 65536], P('code', 'item'), may hold values from -6 to 6
- codebook: float32 [256, 65536], P('item', 'code'), may hold values from -6 to 6
- item_weight: float32 [65536], P('item'), may hold values from 1 to 100
- code_capacity: float32 [65536], P('code'), may hold values from 0.25 to 4
- pairs: int32 [1024, 128], P('item', 'code'), may hold values from -1 to 127, as said below
Outputs:
- item_potential: float32 [65536], P('item')
- code_potential: float32 [65536], P('code')
Inputs may be any that keep to these rules, and one draw needn't show every extreme that they name: `pairs`: each entry is -1 (no candidate) or a code block's number within the code shard of its slot column. Within one item block and one code shard the live entries are distinct, the first slot is always live, and between 1 and 8 are live; some device holds exactly 8 live slots in every item block. Every code block is named by some item block.
All inputs are finite; a program needn't handle non-finite values.
Results may differ from a plain program's by a relative error of at most 0.0003.
Values sent between devices are 32-bit elements; how exact they have to be, the bound alone decides.
A program may use at most 128 MiB of HBM per device.

v0:
```python
import math
import jax
import jax.numpy as jnp
from jax import lax
from jax.sharding import PartitionSpec as P

BLOCK = 64
ITERS = 3
masked_score = -1e30
softness_factor = 0.1


def body(residuals, codebook, item_weight, code_capacity, pairs):
    item_columns = lax.all_gather(residuals, "code", axis=0, tiled=True)
    code_cols = lax.all_gather(codebook, "item", axis=0, tiled=True)
    embedding_width = item_columns.shape[0]
    item_count = item_columns.shape[1]
    code_count = code_cols.shape[1]
    item_blocks = item_count // BLOCK
    code_blocks = code_count // BLOCK
    logit_scale = 1.0 / (softness_factor * math.sqrt(embedding_width))
    weight_sum = lax.psum(jnp.sum(item_weight), "item")
    capacity_sum = lax.psum(jnp.sum(code_capacity), "code")
    item_logmass = jnp.log(item_weight) - jnp.log(weight_sum)
    code_logmass = jnp.log(code_capacity) - jnp.log(capacity_sum)
    is_live = pairs >= 0
    safe_ids = jnp.where(is_live, pairs, 0)
    target = jnp.where(is_live, pairs, code_blocks)
    item_split_cols = item_columns.reshape(embedding_width, item_blocks, BLOCK)
    code_column_splits = code_cols.reshape(embedding_width, code_blocks, BLOCK)
    group = math.gcd(item_blocks, 8)
    group_count = item_blocks // group

    def build_tiles(own, ids, live):
        picked = code_column_splits[:, ids, :]
        scores = (
            jnp.einsum("rbi,rbsj->bsij", own, picked, precision=lax.Precision.HIGHEST) * logit_scale
        )
        return jnp.where(live[:, :, None, None], scores, masked_score)

    reduce_fn = lambda tiles, ids, portion: tiles

    def one_group(group_index):
        start = group_index * group
        own = lax.dynamic_slice_in_dim(item_split_cols, start, group, 1)
        ids = lax.dynamic_slice_in_dim(safe_ids, start, group, 0)
        live = lax.dynamic_slice_in_dim(is_live, start, group, 0)
        portion = lax.dynamic_slice_in_dim(safe_ids, start, group, 0)
        return reduce_fn(build_tiles(own, ids, live), ids, portion)

    results = lax.map(one_group, jnp.arange(group_count, dtype=jnp.int32))
    saved_tile_blocks = results.reshape((item_blocks,) + results.shape[2:])

    def run_pass(reduce_fn, extra):
        return reduce_fn(saved_tile_blocks, safe_ids, extra)

    flat_target = target.reshape(-1)
    flat_rows = flat_target.shape[0]
    row_group = math.gcd(flat_rows, 256)
    one_hot = flat_target[:, None] == jnp.arange(code_blocks, dtype=jnp.int32)[None, :]
    one_hot_groups = one_hot.reshape(flat_rows // row_group, row_group, code_blocks)
    one_hot_float = one_hot.astype(jnp.float32)
    code_potential = jnp.zeros((code_count,), jnp.float32)
    item_potential = jnp.zeros((item_count,), jnp.float32)
    for sweep in range(ITERS):
        code_split = code_potential.reshape(code_blocks, BLOCK)

        def row_reduce(tiles, ids, portion):
            logits = tiles + code_split[ids][:, :, None, :]
            block_peak = jnp.max(logits, axis=(1, 3))
            block_total = jnp.sum(jnp.exp(logits - block_peak[:, None, :, None]), axis=(1, 3))
            return (block_peak, block_total)

        row_peak, row_total = run_pass(row_reduce, safe_ids)
        row_peak = row_peak.reshape(item_count)
        row_total = row_total.reshape(item_count)
        merged_peak = lax.pmax(row_peak, "code")
        merged_total = lax.psum(row_total * jnp.exp(row_peak - merged_peak), "code")
        item_potential = item_logmass - (merged_peak + jnp.log(merged_total))
        item_split = item_potential.reshape(item_blocks, BLOCK)

        def col_reduce(tiles, ids, portion):
            logits = tiles + portion[:, None, :, None]
            block_peak = jnp.max(logits, axis=2)
            block_total = jnp.sum(jnp.exp(logits - block_peak[:, :, None, :]), axis=2)
            return (block_peak, block_total)

        tile_peak, tile_total = run_pass(col_reduce, item_split)
        peak_flat = tile_peak.reshape(flat_rows, BLOCK)
        total_flat = tile_total.reshape(flat_rows, BLOCK)
        peak_groups = peak_flat.reshape(flat_rows // row_group, row_group, BLOCK)

        def peak_step(carry, pieces):
            hot, peaks = pieces
            candidate = jnp.max(jnp.where(hot[:, :, None], peaks[:, None, :], masked_score), axis=0)
            return (jnp.maximum(carry, candidate), None)

        col_peak, unused = lax.scan(
            peak_step,
            jnp.full((code_blocks, BLOCK), masked_score, jnp.float32),
            (one_hot_groups, peak_groups),
        )
        padded_peak = jnp.concatenate(
            [col_peak, jnp.full((1, BLOCK), masked_score, jnp.float32)], axis=0
        )
        spread = total_flat * jnp.exp(peak_flat - padded_peak[flat_target])
        col_total = jnp.dot(
            one_hot_float.T,
            spread,
            precision=lax.Precision.HIGHEST,
            preferred_element_type=jnp.float32,
        )
        col_peak = col_peak.reshape(code_count)
        col_total = col_total.reshape(code_count)
        joined_peak = lax.pmax(col_peak, "item")
        joined_total = lax.psum(col_total * jnp.exp(col_peak - joined_peak), "item")
        code_potential = code_logmass - (joined_peak + jnp.log(joined_total))
    return (item_potential, code_potential)


def solution(mesh):
    placed = (P("code", "item"), P("item", "code"), P("item"), P("code"), P("item", "code"))
    return jax.shard_map(
        body, mesh=mesh, in_specs=placed, out_specs=(P("item"), P("code")), check_vma=False
    )
```

profile of v0, /device:TPU:0, one launch (start us, length us, event | category | flops | bytes accessed | tf_op | source)
XLA Modules:
  0.0 1095.6 jit_solution(9727637983515556993)
XLA Ops:
  10.0 42.6 %psum.56 = f32[]{:T(128)} all-reduce(f32[]{:T(128)} %reduce_sum.72), channel_id=1, replica_groups=mesh['item'=16,'code'=8] {'item'}, use_global_device_ids=true, to_apply=%region_1.0 | all-reduce | flops 1 | bytes 8 | tf_op jit(solution)/shard_map/psum | solution.py:22
  58.9 5.6 copy.31
  64.6 52.7 %all-gather.3.cloned.1.call-done = f32[256,8192]{1,0:T(8,128)} async-done(((f32[16,8192]{1,0:T(8,128)}), f32[256,8192]{1,0:T(8,128)}) %all-gather.3.cloned.1.call-update) | async-done | bytes 8388624 | tf_op jit(solution)/shard_map/all_gather | solution.py:15
  117.3 9.0 copy.30
  126.3 158.7 %while.43 = (s32[]{:T(128)}, f32[8,8,16,64,64]{3,4,2,1,0:T(8,128)}, s32[8]{0:T(128)S(1)}, pred[64,16]{1,0:T(8,128)(4,1)S(1)}, s32[64,16]{1,0:T(8,128)S(1)}, /*in...) while((s32[]{:T(128)}, f32[8,8,16,64,64]{3,4,2,1,0:T(8,128)}, ...), condition=%wide.region_3.0_spmd, body=%wide.region_2.0_spmd.sunk | while | flops 1611662720 | bytes 29892660 | solution.py:51
  127.5 7.7 gather_fusion
  135.2 11.0 bitcast_dynamic-update-slice_fusion.2
  147.3 7.7 gather_fusion
  155.0 11.0 %bitcast_dynamic-update-slice_fusion.2 = f32[8,8,16,64,64]{3,4,2,1,0:T(8,128)} fusion(f32[8,8,16,64,64]{3,4,2,1,0:T(8,128)} %get-tuple-element.327, s32[]{:T(128)} %get-tuple-element.326, f32[256,8,16,64]{0,3,2,1:T(8,128)} %bitcast.84, pred[8,16]{1,0:T(8,128)(4,1)S(1)} %constant_dynamic-slice_fusion.2, f32[256,64,64]{0,2,1:T(8,128)} %get-tuple-element.343, ...), kind=kOutput, calls=%fused_computation.7.clone.1 | convolution fusion | flops 1611661312 | bytes 13107844 | tf_op jit(solution)/shard_map/while/body/eval_jaxpr/rbi,rbsj->bsij/dot_general | solution.py:37
  167.2 7.7 gather_fusion
  174.8 10.9 bitcast_dynamic-update-slice_fusion.2
  187.0 7.7 gather_fusion
  194.7 10.9 bitcast_dynamic-update-slice_fusion.2
  206.8 7.7 gather_fusion
  214.5 11.0 bitcast_dynamic-update-slice_fusion.2
  226.7 7.7 gather_fusion
  234.3 11.0 %bitcast_dynamic-update-slice_fusion.2 = f32[8,8,16,64,64]{3,4,2,1,0:T(8,128)} fusion(f32[8,8,16,64,64]{3,4,2,1,0:T(8,128)} %get-tuple-element.327, s32[]{:T(128)} %get-tuple-element.326, f32[256,8,16,64]{0,3,2,1:T(8,128)} %bitcast.84, pred[8,16]{1,0:T(8,128)(4,1)S(1)} %constant_dynamic-slice_fusion.2, f32[256,64,64]{0,2,1:T(8,128)} %get-tuple-element.343, ...), kind=kOutput, calls=%fused_computation.7.clone.1 | convolution fusion | flops 1611661312 | bytes 13107844 | tf_op jit(solution)/shard_map/while/body/eval_jaxpr/rbi,rbsj->bsij/dot_general | solution.py:37
  246.5 7.7 gather_fusion
  254.2 10.9 bitcast_dynamic-update-slice_fusion.2
  266.3 7.7 gather_fusion
  274.0 11.0 %bitcast_dynamic-update-slice_fusion.2 = f32[8,8,16,64,64]{3,4,2,1,0:T(8,128)} fusion(f32[8,8,16,64,64]{3,4,2,1,0:T(8,128)} %get-tuple-element.327, s32[]{:T(128)} %get-tuple-element.326, f32[256,8,16,64]{0,3,2,1:T(8,128)} %bitcast.84, pred[8,16]{1,0:T(8,128)(4,1)S(1)} %constant_dynamic-slice_fusion.2, f32[256,64,64]{0,2,1:T(8,128)} %get-tuple-element.343, ...), kind=kOutput, calls=%fused_computation.7.clone.1 | convolution fusion | flops 1611661312 | bytes 13107844 | tf_op jit(solution)/shard_map/while/body/eval_jaxpr/rbi,rbsj->bsij/dot_general | solution.py:37
  285.0 11.8 %add_reduce_fusion.5 = f32[8,8,64]{2,1,0:T(8,128)S(1)} fusion(f32[8,8,16,64,64]{3,4,2,1,0:T(8,128)} %get-tuple-element.105, f32[8,8,16,64]{3,2,1,0:T(8,128)S(1)} %bitcast.93), kind=kLoop, calls=%fused_computation.37 | loop fusion | flops 8384512 | bytes 17055744 | tf_op jit(solution)/shard_map/reduce_max | solution.py:70
  296.8 11.9 %exponential_reduce_fusion.5 = f32[8,8,64]{2,1,0:T(8,128)S(1)} fusion(f32[8,8,16,64,64]{3,4,2,1,0:T(8,128)} %get-tuple-element.105, f32[8,8,64]{2,1,0:T(8,128)S(1)} %add_reduce_fusion.5, f32[8,8,16,64]{3,2,1,0:T(8,128)S(1)} %bitcast.94), kind=kLoop, calls=%fused_computation.31 | loop fusion | flops 12578816 | bytes 17072128 | tf_op jit(solution)/shard_map/reduce_sum | solution.py:71
  308.9 25.5 %pmax.42 = f32[4096]{0:T(1024)S(1)} all-reduce(f32[4096]{0:T(1024)S(1)} %reshape.211), channel_id=1, replica_groups=mesh['item'=16,'code'=8] {'code'}, use_global_device_ids=true, to_apply=%region_7.8 | all-reduce | flops 4096 | bytes 32768 | tf_op jit(solution)/shard_map/pmax | solution.py:77
  334.4 24.6 %all-reduce.3 = (f32[4096]{0:T(1024)S(1)}, f32[]{:T(128)}) all-reduce(f32[4096]{0:T(1024)S(1)} %exponential_multiply_fusion.5, f32[]{:T(128)} %reduce_sum.73), channel_id=1, replica_groups=mesh['item'=16,'code'=8] {'code'}, use_global_device_ids=true, to_apply=%region_9.10 | all-reduce | flops 4097 | bytes 32776 | tf_op jit(solution)/shard_map/psum | solution.py:78
  359.1 15.3 %add_reduce_fusion.4 = f32[8,8,16,64]{3,2,1,0:T(8,128)S(1)} fusion(f32[8,8,16,64,64]{3,4,2,1,0:T(8,128)} %get-tuple-element.105, f32[8,8,64]{2,1,0:T(8,128)S(1)} %add.154), kind=kLoop, calls=%fused_computation.36 | loop fusion | flops 8323072 | bytes 17055744 | tf_op jit(solution)/shard_map/reduce_max | solution.py:84
  374.4 20.7 %exponential_reduce_fusion.4 = f32[8,8,16,64]{3,2,1,0:T(8,128)S(1)} fusion(f32[8,8,16,64,64]{3,4,2,1,0:T(8,128)} %get-tuple-element.105, f32[8,8,16,64]{3,2,1,0:T(8,128)S(1)} %add_reduce_fusion.4, f32[8,8,64]{2,1,0:T(8,128)S(1)} %add.154), kind=kLoop, calls=%fused_computation.30 | loop fusion | flops 12517376 | bytes 17317888 | tf_op jit(solution)/shard_map/reduce_sum | solution.py:85
  395.1 13.3 %while.44 = (s32[]{:T(128)}, f32[128,64]{0,1:T(8,128)S(1)}, pred[4,256,128]{2,1,0:T(8,128)(4,1)S(1)}, f32[4,256,64]{2,1,0:T(8,128)S(1)}, s32[]{:T(128)}, /*index=5*/s32[]{:T(128)}) while((s32[]{:T(128)}, f32[128,64]{0,1:T(8,128)S(1)}, pred[4,256,128]{2,1,0:T(8,128)(4,1)S(1)}, f32[4,256,64]{2,1,0:T(8,128)S(1)}, s32[]{:T(128)}, ...), condition=%wide.region_13.14_spmd.clone, body=%wide.region_11.13_spmd.clone.sunk | while | flops 4202499 | bytes 426071 | solution.py:98
  412.4 72.4 %pmax.43 = f32[8192]{0:T(1024)S(1)} all-reduce(f32[8192]{0:T(1024)S(1)} %reshape.213), channel_id=1, replica_groups=mesh['item'=16,'code'=8] {'item'}, use_global_device_ids=true, to_apply=%region_14.15 | all-reduce | flops 8192 | bytes 65536 | tf_op jit(solution)/shard_map/pmax | solution.py:115
  484.8 69.5 %psum.59 = f32[8192]{0:T(1024)S(1)} all-reduce(f32[8192]{0:T(1024)S(1)} %exponential_multiply_fusion.2), channel_id=1, replica_groups=mesh['item'=16,'code'=8] {'item'}, use_global_device_ids=true, to_apply=%region_16.17 | all-reduce | flops 8192 | bytes 65536 | tf_op jit(solution)/shard_map/psum | solution.py:116
  558.0 11.8 %add_reduce_fusion.3 = f32[8,8,64]{2,1,0:T(8,128)S(1)} fusion(f32[8,8,16,64,64]{3,4,2,1,0:T(8,128)} %get-tuple-element.105, f32[8,8,16,64]{3,2,1,0:T(8,128)S(1)} %bitcast.97), kind=kLoop, calls=%fused_computation.35 | loop fusion | flops 8384512 | bytes 17055744 | tf_op jit(solution)/shard_map/reduce_max | solution.py:70
  569.8 11.9 %exponential_reduce_fusion.3 = f32[8,8,64]{2,1,0:T(8,128)S(1)} fusion(f32[8,8,16,64,64]{3,4,2,1,0:T(8,128)} %get-tuple-element.105, f32[8,8,64]{2,1,0:T(8,128)S(1)} %add_reduce_fusion.3, f32[8,8,16,64]{3,2,1,0:T(8,128)S(1)} %bitcast.98), kind=kLoop, calls=%fused_computation.29 | loop fusion | flops 12578816 | bytes 17072128 | tf_op jit(solution)/shard_map/reduce_sum | solution.py:71
  581.9 23.5 %pmax.44 = f32[4096]{0:T(1024)S(1)} all-reduce(f32[4096]{0:T(1024)S(1)} %reshape.219), channel_id=1, replica_groups=mesh['item'=16,'code'=8] {'code'}, use_global_device_ids=true, to_apply=%region_18.19 | all-reduce | flops 4096 | bytes 32768 | tf_op jit(solution)/shard_map/pmax | solution.py:77
  605.4 23.6 %psum.60 = f32[4096]{0:T(1024)S(1)} all-reduce(f32[4096]{0:T(1024)S(1)} %exponential_multiply_fusion.4), channel_id=1, replica_groups=mesh['item'=16,'code'=8] {'code'}, use_global_device_ids=true, to_apply=%region_20.21 | all-reduce | flops 4096 | bytes 32768 | tf_op jit(solution)/shard_map/psum | solution.py:78
  629.1 15.3 %add_reduce_fusion.2 = f32[8,8,16,64]{3,2,1,0:T(8,128)S(1)} fusion(f32[8,8,16,64,64]{3,4,2,1,0:T(8,128)} %get-tuple-element.105, f32[8,8,64]{2,1,0:T(8,128)S(1)} %add.163), kind=kLoop, calls=%fused_computation.34 | loop fusion | flops 8323072 | bytes 17055744 | tf_op jit(solution)/shard_map/reduce_max | solution.py:84
  644.4 20.7 %exponential_reduce_fusion.2 = f32[8,8,16,64]{3,2,1,0:T(8,128)S(1)} fusion(f32[8,8,16,64,64]{3,4,2,1,0:T(8,128)} %get-tuple-element.105, f32[8,8,16,64]{3,2,1,0:T(8,128)S(1)} %add_reduce_fusion.2, f32[8,8,64]{2,1,0:T(8,128)S(1)} %add.163), kind=kLoop, calls=%fused_computation.28 | loop fusion | flops 12517376 | bytes 17317888 | tf_op jit(solution)/shard_map/reduce_sum | solution.py:85
  665.0 13.3 %while.45 = (s32[]{:T(128)}, f32[128,64]{0,1:T(8,128)S(1)}, pred[4,256,128]{2,1,0:T(8,128)(4,1)S(1)}, f32[4,256,64]{2,1,0:T(8,128)S(1)}, s32[]{:T(128)}, /*index=5*/s32[]{:T(128)}) while((s32[]{:T(128)}, f32[128,64]{0,1:T(8,128)S(1)}, pred[4,256,128]{2,1,0:T(8,128)(4,1)S(1)}, f32[4,256,64]{2,1,0:T(8,128)S(1)}, s32[]{:T(128)}, ...), condition=%wide.region_24.25_spmd.clone, body=%wide.region_22.24_spmd.clone.sunk | while | flops 4202499 | bytes 426071 | solution.py:98
  682.3 69.6 %pmax.45 = f32[8192]{0:T(1024)S(1)} all-reduce(f32[8192]{0:T(1024)S(1)} %reshape.221), channel_id=1, replica_groups=mesh['item'=16,'code'=8] {'item'}, use_global_device_ids=true, to_apply=%region_25.26 | all-reduce | flops 8192 | bytes 65536 | tf_op jit(solution)/shard_map/pmax | solution.py:115
  751.9 69.5 %psum.61 = f32[8192]{0:T(1024)S(1)} all-reduce(f32[8192]{0:T(1024)S(1)} %exponential_multiply_fusion.1), channel_id=1, replica_groups=mesh['item'=16,'code'=8] {'item'}, use_global_device_ids=true, to_apply=%region_27.28 | all-reduce | flops 8192 | bytes 65536 | tf_op jit(solution)/shard_map/psum | solution.py:116
  824.4 11.8 %add_reduce_fusion.1 = f32[8,8,64]{2,1,0:T(8,128)S(1)} fusion(f32[8,8,16,64,64]{3,4,2,1,0:T(8,128)} %get-tuple-element.105, f32[8,8,16,64]{3,2,1,0:T(8,128)S(1)} %bitcast.95), kind=kLoop, calls=%fused_computation.33 | loop fusion | flops 8384512 | bytes 17055744 | tf_op jit(solution)/shard_map/reduce_max | solution.py:70
  836.2 11.9 %exponential_reduce_fusion.1 = f32[8,8,64]{2,1,0:T(8,128)S(1)} fusion(f32[8,8,16,64,64]{3,4,2,1,0:T(8,128)} %get-tuple-element.105, f32[8,8,64]{2,1,0:T(8,128)S(1)} %add_reduce_fusion.1, f32[8,8,16,64]{3,2,1,0:T(8,128)S(1)} %bitcast.96), kind=kLoop, calls=%fused_computation.27 | loop fusion | flops 12578816 | bytes 17072128 | tf_op jit(solution)/shard_map/reduce_sum | solution.py:71
  848.3 23.5 %pmax.46 = f32[4096]{0:T(1024)S(1)} all-reduce(f32[4096]{0:T(1024)S(1)} %reshape.226), channel_id=1, replica_groups=mesh['item'=16,'code'=8] {'code'}, use_global_device_ids=true, to_apply=%region_29.30 | all-reduce | flops 4096 | bytes 32768 | tf_op jit(solution)/shard_map/pmax | solution.py:77
  871.8 23.8 %psum.62 = f32[4096]{0:T(1024)S(1)} all-reduce(f32[4096]{0:T(1024)S(1)} %exponential_multiply_fusion.3), channel_id=1, replica_groups=mesh['item'=16,'code'=8] {'code'}, use_global_device_ids=true, to_apply=%region_31.32 | all-reduce | flops 4096 | bytes 32768 | tf_op jit(solution)/shard_map/psum | solution.py:78
  895.7 15.3 %add_reduce_fusion = f32[8,8,16,64]{3,2,1,0:T(8,128)S(1)} fusion(f32[8,8,16,64,64]{3,4,2,1,0:T(8,128)} %get-tuple-element.105, f32[8,8,64]{2,1,0:T(8,128)S(1)} %add.171), kind=kLoop, calls=%fused_computation.32 | loop fusion | flops 8323072 | bytes 17055744 | tf_op jit(solution)/shard_map/reduce_max | solution.py:84
  911.0 20.7 %exponential_reduce_fusion = f32[8,8,16,64]{3,2,1,0:T(8,128)S(1)} fusion(f32[8,8,16,64,64]{3,4,2,1,0:T(8,128)} %get-tuple-element.105, f32[8,8,16,64]{3,2,1,0:T(8,128)S(1)} %add_reduce_fusion, f32[8,8,64]{2,1,0:T(8,128)S(1)} %add.171), kind=kLoop, calls=%fused_computation.26 | loop fusion | flops 12517376 | bytes 17317888 | tf_op jit(solution)/shard_map/reduce_sum | solution.py:85
  931.7 13.3 %while.46 = (s32[]{:T(128)}, f32[128,64]{0,1:T(8,128)S(1)}, pred[4,256,128]{2,1,0:T(8,128)(4,1)S(1)}, f32[4,256,64]{2,1,0:T(8,128)S(1)}, s32[]{:T(128)}, /*index=5*/s32[]{:T(128)}) while((s32[]{:T(128)}, f32[128,64]{0,1:T(8,128)S(1)}, pred[4,256,128]{2,1,0:T(8,128)(4,1)S(1)}, f32[4,256,64]{2,1,0:T(8,128)S(1)}, s32[]{:T(128)}, ...), condition=%wide.region_35.36_spmd.clone, body=%wide.region_33.35_spmd.clone.sunk | while | flops 4202499 | bytes 426071 | solution.py:98
  948.9 69.6 %pmax.47 = f32[8192]{0:T(1024)S(1)} all-reduce(f32[8192]{0:T(1024)S(1)} %reshape.228), channel_id=1, replica_groups=mesh['item'=16,'code'=8] {'item'}, use_global_device_ids=true, to_apply=%region_36.37 | all-reduce | flops 8192 | bytes 65536 | tf_op jit(solution)/shard_map/pmax | solution.py:115
  1018.5 69.5 %psum.63 = f32[8192]{0:T(1024)S(1)} all-reduce(f32[8192]{0:T(1024)S(1)} %exponential_multiply_fusion), channel_id=1, replica_groups=mesh['item'=16,'code'=8] {'item'}, use_global_device_ids=true, to_apply=%region_38.39 | all-reduce | flops 8192 | bytes 65536 | tf_op jit(solution)/shard_map/psum | solution.py:116
  (169 shorter events, 71.9 us)
Async XLA Ops:
  7.2 51.8 %all-gather.5.cloned.1.call-start = ((), (), s32[]{:S(2)}) async-start(), calls=%async_computation.1 | async-start | bytes 4718592 | tf_op jit(solution)/shard_map/all_gather | solution.py:14
  7.9 109.4 %all-gather.3.cloned.1.call-start = ((), (), s32[]{:S(2)}) async-start(), calls=%async_computation | async-start | bytes 8912896 | tf_op jit(solution)/shard_map/all_gather | solution.py:15
  285.0 74.0 %copy-start.3 = (f32[4096]{0:T(1024)S(1)}, f32[4096]{0:T(1024)}, u32[]{:S(2)}) copy-start(f32[4096]{0:T(1024)} %param.15) | copy-start | bytes 49156
  359.1 195.9 %copy-start.2 = (f32[8192]{0:T(1024)S(1)}, f32[8192]{0:T(1024)}, u32[]{:S(2)}) copy-start(f32[8192]{0:T(1024)} %param.16) | copy-start | bytes 98308
  629.1 36.0 %copy-start.1 = (f32[128,64]{0,1:T(8,128)S(1)}, f32[128,64]{0,1:T(8,128)}, u32[]{:S(2)}) copy-start(f32[128,64]{0,1:T(8,128)} %custom-call.1) | copy-start | bytes 98308
  895.6 36.1 %copy-start.4 = (f32[4096]{0:T(1024)}, f32[4096]{0:T(1024)S(1)}, u32[]{:S(2)}) copy-start(f32[4096]{0:T(1024)S(1)} %add_subtract_fusion.3) | copy-start | bytes 49156
  895.7 36.0 %copy-start = (f32[128,64]{0,1:T(8,128)S(1)}, f32[128,64]{0,1:T(8,128)}, u32[]{:S(2)}) copy-start(f32[128,64]{0,1:T(8,128)} %custom-call.2) | copy-start | bytes 98308
Sparse Core Ops, SparseCore 0:
  9.7 34.5 all-gather.4
  46.4 70.8 all-gather.2
where the time goes:
time: 1100 us
  blocking collectives  607 us (55%)
  other arithmetic  222 us (20%)
  local copies, waits for them, and re-layouts  101 us (9%)
  matrix products  89.9 us (8%)
  waiting for transfers between devices  54.1 us (5%)
  between operations  15.8 us (1%)
    pmax x3, blocking collectives, body(): joined_peak = lax.pmax(col_peak, 'item')  212 us
    psum x3, blocking collectives, body(): joined_total = lax.psum(col_total * jnp.exp(col_peak - joined_peak), 'item')  209 us
    dot_general x8, matrix products, build_tiles(): jnp.einsum('rbi,rbsj->bsij', own, picked, precision=lax.Precision.HIGHEST)  87.6 us
    pmax x3, blocking collectives, body(): merged_peak = lax.pmax(row_peak, 'code')  72.6 us
    psum x3, blocking collectives, body(): merged_total = lax.psum(row_total * jnp.exp(row_peak - merged_peak), 'code')  71.9 us
    reduce_sum x3, other arithmetic, col_reduce(): block_total = jnp.sum(jnp.exp(logits - block_peak[:, :, None, :]), axis=2)  62 us
    gather x8, local copies, waits for them, and re-layouts, build_tiles(): picked = code_column_splits[:, ids, :]  61.3 us
    all_gather x1, waiting for transfers between devices, body(): code_cols = lax.all_gather(codebook, 'item', axis=0, tiled=True)  52.7 us
  transfers between devices with their start and end apart: 2, of which 1 were waited for; matrix products, arithmetic and copies ran while one was open for 1% of the time, Pallas kernels for 0%

commit v1 on v0

--- a/solution.py
+++ b/solution.py
@@ -113,7 +113,9 @@
         col_peak = col_peak.reshape(code_count)
         col_total = col_total.reshape(code_count)
         joined_peak = lax.pmax(col_peak, "item")
-        joined_total = lax.psum(col_total * jnp.exp(col_peak - joined_peak), "item")
+        joined_total = jnp.sum(
+            lax.all_gather(col_total * jnp.exp(col_peak - joined_peak), "item"), axis=0
+        )
         code_potential = code_logmass - (joined_peak + jnp.log(joined_total))
     return (item_potential, code_potential)
 

time: 1100 us -> 957 us (0.87)
  blocking collectives: 607 us -> 466 us
    psum x3 -> x0, blocking collectives: 209 us -> none  [body(): joined_total = lax.psum(col_total * jnp.exp(col_peak - joined_peak), 'item')]
    all_gather x0 -> x3, blocking collectives: none -> 62.8 us  [body(): lax.all_gather(col_total * jnp.exp(col_peak - joined_peak), 'item')]
where the time goes in v1:
time: 957 us; the launch traced here: 955 us
  blocking collectives  466 us (49%)
  other arithmetic  223 us (23%)
  local copies, waits for them, and re-layouts  101 us (11%)
  matrix products  89.9 us (9%)
  waiting for transfers between devices  54.1 us (6%)
  between operations  15.8 us (2%)
    pmax x3, blocking collectives, body(): joined_peak = lax.pmax(col_peak, 'item')  217 us
    dot_general x8, matrix products, build_tiles(): jnp.einsum('rbi,rbsj->bsij', own, picked, precision=lax.Precision.HIGHEST)  87.6 us
    pmax x3, blocking collectives, body(): merged_peak = lax.pmax(row_peak, 'code')  72.6 us
    psum x3, blocking collectives, body(): merged_total = lax.psum(row_total * jnp.exp(row_peak - merged_peak), 'code')  71.9 us
    all_gather x3, blocking collectives, body(): lax.all_gather(col_total * jnp.exp(col_peak - joined_peak), 'item')  62.8 us
    reduce_sum x3, other arithmetic, col_reduce(): block_total = jnp.sum(jnp.exp(logits - block_peak[:, :, None, :]), axis=2)  62 us
    gather x8, local copies, waits for them, and re-layouts, build_tiles(): picked = code_column_splits[:, ids, :]  61.3 us
    all_gather x1, waiting for transfers between devices, body(): code_cols = lax.all_gather(codebook, 'item', axis=0, tiled=True)  52.7 us
  transfers between devices with their start and end apart: 2, of which 1 were waited for; matrix products, arithmetic and copies ran while one was open for 1% of the time, Pallas kernels for 0%

profile of v1, /device:TPU:0, one launch (start us, length us, event | category | flops | bytes accessed | tf_op | source)
XLA Modules:
  0.0 955.2 jit_solution(13780159387268010133)
XLA Ops:
  10.0 42.6 %psum.35 = f32[]{:T(128)} all-reduce(f32[]{:T(128)} %reduce_sum.99), channel_id=1, replica_groups=mesh['item'=16,'code'=8] {'item'}, use_global_device_ids=true, to_apply=%region_1.0 | all-reduce | flops 1 | bytes 8 | tf_op jit(solution)/shard_map/psum | solution.py:22
  58.9 5.6 copy.31
  64.6 52.7 %all-gather.6.cloned.1.call-done = f32[256,8192]{1,0:T(8,128)} async-done(((f32[16,8192]{1,0:T(8,128)}), f32[256,8192]{1,0:T(8,128)}) %all-gather.6.cloned.1.call-update) | async-done | bytes 8388624 | tf_op jit(solution)/shard_map/all_gather | solution.py:15
  117.3 9.0 copy.30
  126.3 158.7 %while.43 = (s32[]{:T(128)}, f32[8,8,16,64,64]{3,4,2,1,0:T(8,128)}, s32[8]{0:T(128)S(1)}, pred[64,16]{1,0:T(8,128)(4,1)S(1)}, s32[64,16]{1,0:T(8,128)S(1)}, /*in...) while((s32[]{:T(128)}, f32[8,8,16,64,64]{3,4,2,1,0:T(8,128)}, ...), condition=%wide.region_3.0_spmd, body=%wide.region_2.0_spmd.sunk | while | flops 1611662720 | bytes 29892660 | solution.py:51
  127.5 7.7 gather_fusion
  135.2 11.0 %bitcast_dynamic-update-slice_fusion.2 = f32[8,8,16,64,64]{3,4,2,1,0:T(8,128)} fusion(f32[8,8,16,64,64]{3,4,2,1,0:T(8,128)} %get-tuple-element.327, s32[]{:T(128)} %get-tuple-element.326, f32[256,8,16,64]{0,3,2,1:T(8,128)} %bitcast.84, pred[8,16]{1,0:T(8,128)(4,1)S(1)} %constant_dynamic-slice_fusion.2, f32[256,64,64]{0,2,1:T(8,128)} %get-tuple-element.343, ...), kind=kOutput, calls=%fused_computation.7.clone.1 | convolution fusion | flops 1611661312 | bytes 13107844 | tf_op jit(solution)/shard_map/while/body/eval_jaxpr/rbi,rbsj->bsij/dot_general | solution.py:37
  147.3 7.7 gather_fusion
  155.0 11.0 %bitcast_dynamic-update-slice_fusion.2 = f32[8,8,16,64,64]{3,4,2,1,0:T(8,128)} fusion(f32[8,8,16,64,64]{3,4,2,1,0:T(8,128)} %get-tuple-element.327, s32[]{:T(128)} %get-tuple-element.326, f32[256,8,16,64]{0,3,2,1:T(8,128)} %bitcast.84, pred[8,16]{1,0:T(8,128)(4,1)S(1)} %constant_dynamic-slice_fusion.2, f32[256,64,64]{0,2,1:T(8,128)} %get-tuple-element.343, ...), kind=kOutput, calls=%fused_computation.7.clone.1 | convolution fusion | flops 1611661312 | bytes 13107844 | tf_op jit(solution)/shard_map/while/body/eval_jaxpr/rbi,rbsj->bsij/dot_general | solution.py:37
  167.2 7.7 gather_fusion
  174.8 10.9 %bitcast_dynamic-update-slice_fusion.2 = f32[8,8,16,64,64]{3,4,2,1,0:T(8,128)} fusion(f32[8,8,16,64,64]{3,4,2,1,0:T(8,128)} %get-tuple-element.327, s32[]{:T(128)} %get-tuple-element.326, f32[256,8,16,64]{0,3,2,1:T(8,128)} %bitcast.84, pred[8,16]{1,0:T(8,128)(4,1)S(1)} %constant_dynamic-slice_fusion.2, f32[256,64,64]{0,2,1:T(8,128)} %get-tuple-element.343, ...), kind=kOutput, calls=%fused_computation.7.clone.1 | convolution fusion | flops 1611661312 | bytes 13107844 | tf_op jit(solution)/shard_map/while/body/eval_jaxpr/rbi,rbsj->bsij/dot_general | solution.py:37
  187.0 7.7 gather_fusion
  194.7 10.9 %bitcast_dynamic-update-slice_fusion.2 = f32[8,8,16,64,64]{3,4,2,1,0:T(8,128)} fusion(f32[8,8,16,64,64]{3,4,2,1,0:T(8,128)} %get-tuple-element.327, s32[]{:T(128)} %get-tuple-element.326, f32[256,8,16,64]{0,3,2,1:T(8,128)} %bitcast.84, pred[8,16]{1,0:T(8,128)(4,1)S(1)} %constant_dynamic-slice_fusion.2, f32[256,64,64]{0,2,1:T(8,128)} %get-tuple-element.343, ...), kind=kOutput, calls=%fused_computation.7.clone.1 | convolution fusion | flops 1611661312 | bytes 13107844 | tf_op jit(solution)/shard_map/while/body/eval_jaxpr/rbi,rbsj->bsij/dot_general | solution.py:37
  206.8 7.7 gather_fusion
  214.5 11.0 %bitcast_dynamic-update-slice_fusion.2 = f32[8,8,16,64,64]{3,4,2,1,0:T(8,128)} fusion(f32[8,8,16,64,64]{3,4,2,1,0:T(8,128)} %get-tuple-element.327, s32[]{:T(128)} %get-tuple-element.326, f32[256,8,16,64]{0,3,2,1:T(8,128)} %bitcast.84, pred[8,16]{1,0:T(8,128)(4,1)S(1)} %constant_dynamic-slice_fusion.2, f32[256,64,64]{0,2,1:T(8,128)} %get-tuple-element.343, ...), kind=kOutput, calls=%fused_computation.7.clone.1 | convolution fusion | flops 1611661312 | bytes 13107844 | tf_op jit(solution)/shard_map/while/body/eval_jaxpr/rbi,rbsj->bsij/dot_general | solution.py:37
  226.7 7.7 gather_fusion
  234.3 11.0 %bitcast_dynamic-update-slice_fusion.2 = f32[8,8,16,64,64]{3,4,2,1,0:T(8,128)} fusion(f32[8,8,16,64,64]{3,4,2,1,0:T(8,128)} %get-tuple-element.327, s32[]{:T(128)} %get-tuple-element.326, f32[256,8,16,64]{0,3,2,1:T(8,128)} %bitcast.84, pred[8,16]{1,0:T(8,128)(4,1)S(1)} %constant_dynamic-slice_fusion.2, f32[256,64,64]{0,2,1:T(8,128)} %get-tuple-element.343, ...), kind=kOutput, calls=%fused_computation.7.clone.1 | convolution fusion | flops 1611661312 | bytes 13107844 | tf_op jit(solution)/shard_map/while/body/eval_jaxpr/rbi,rbsj->bsij/dot_general | solution.py:37
  246.5 7.7 gather_fusion
  254.2 10.9 %bitcast_dynamic-update-slice_fusion.2 = f32[8,8,16,64,64]{3,4,2,1,0:T(8,128)} fusion(f32[8,8,16,64,64]{3,4,2,1,0:T(8,128)} %get-tuple-element.327, s32[]{:T(128)} %get-tuple-element.326, f32[256,8,16,64]{0,3,2,1:T(8,128)} %bitcast.84, pred[8,16]{1,0:T(8,128)(4,1)S(1)} %constant_dynamic-slice_fusion.2, f32[256,64,64]{0,2,1:T(8,128)} %get-tuple-element.343, ...), kind=kOutput, calls=%fused_computation.7.clone.1 | convolution fusion | flops 1611661312 | bytes 13107844 | tf_op jit(solution)/shard_map/while/body/eval_jaxpr/rbi,rbsj->bsij/dot_general | solution.py:37
  266.3 7.7 gather_fusion
  274.0 11.0 %bitcast_dynamic-update-slice_fusion.2 = f32[8,8,16,64,64]{3,4,2,1,0:T(8,128)} fusion(f32[8,8,16,64,64]{3,4,2,1,0:T(8,128)} %get-tuple-element.327, s32[]{:T(128)} %get-tuple-element.326, f32[256,8,16,64]{0,3,2,1:T(8,128)} %bitcast.84, pred[8,16]{1,0:T(8,128)(4,1)S(1)} %constant_dynamic-slice_fusion.2, f32[256,64,64]{0,2,1:T(8,128)} %get-tuple-element.343, ...), kind=kOutput, calls=%fused_computation.7.clone.1 | convolution fusion | flops 1611661312 | bytes 13107844 | tf_op jit(solution)/shard_map/while/body/eval_jaxpr/rbi,rbsj->bsij/dot_general | solution.py:37
  285.0 11.8 %add_reduce_fusion.5 = f32[8,8,64]{2,1,0:T(8,128)S(1)} fusion(f32[8,8,16,64,64]{3,4,2,1,0:T(8,128)} %get-tuple-element.105, f32[8,8,16,64]{3,2,1,0:T(8,128)S(1)} %bitcast.93), kind=kLoop, calls=%fused_computation.37 | loop fusion | flops 8384512 | bytes 17055744 | tf_op jit(solution)/shard_map/reduce_max | solution.py:70
  296.8 11.9 %exponential_reduce_fusion.5 = f32[8,8,64]{2,1,0:T(8,128)S(1)} fusion(f32[8,8,16,64,64]{3,4,2,1,0:T(8,128)} %get-tuple-element.105, f32[8,8,64]{2,1,0:T(8,128)S(1)} %add_reduce_fusion.5, f32[8,8,16,64]{3,2,1,0:T(8,128)S(1)} %bitcast.94), kind=kLoop, calls=%fused_computation.31 | loop fusion | flops 12578816 | bytes 17072128 | tf_op jit(solution)/shard_map/reduce_sum | solution.py:71
  308.9 25.5 %pmax.42 = f32[4096]{0:T(1024)S(1)} all-reduce(f32[4096]{0:T(1024)S(1)} %reshape.211), channel_id=1, replica_groups=mesh['item'=16,'code'=8] {'code'}, use_global_device_ids=true, to_apply=%region_7.8 | all-reduce | flops 4096 | bytes 32768 | tf_op jit(solution)/shard_map/pmax | solution.py:77
  334.4 24.6 %all-reduce.3 = (f32[4096]{0:T(1024)S(1)}, f32[]{:T(128)}) all-reduce(f32[4096]{0:T(1024)S(1)} %exponential_multiply_fusion.5, f32[]{:T(128)} %reduce_sum.100), channel_id=1, replica_groups=mesh['item'=16,'code'=8] {'code'}, use_global_device_ids=true, to_apply=%region_9.10 | all-reduce | flops 4097 | bytes 32776 | tf_op jit(solution)/shard_map/psum | solution.py:78
  359.1 15.3 %add_reduce_fusion.4 = f32[8,8,16,64]{3,2,1,0:T(8,128)S(1)} fusion(f32[8,8,16,64,64]{3,4,2,1,0:T(8,128)} %get-tuple-element.105, f32[8,8,64]{2,1,0:T(8,128)S(1)} %add.148), kind=kLoop, calls=%fused_computation.36 | loop fusion | flops 8323072 | bytes 17055744 | tf_op jit(solution)/shard_map/reduce_max | solution.py:84
  374.4 20.7 %exponential_reduce_fusion.4 = f32[8,8,16,64]{3,2,1,0:T(8,128)S(1)} fusion(f32[8,8,16,64,64]{3,4,2,1,0:T(8,128)} %get-tuple-element.105, f32[8,8,16,64]{3,2,1,0:T(8,128)S(1)} %add_reduce_fusion.4, f32[8,8,64]{2,1,0:T(8,128)S(1)} %add.148), kind=kLoop, calls=%fused_computation.30 | loop fusion | flops 12517376 | bytes 17317888 | tf_op jit(solution)/shard_map/reduce_sum | solution.py:85
  395.1 13.3 %while.44 = (s32[]{:T(128)}, f32[128,64]{0,1:T(8,128)S(1)}, pred[4,256,128]{2,1,0:T(8,128)(4,1)S(1)}, f32[4,256,64]{2,1,0:T(8,128)S(1)}, s32[]{:T(128)}, /*index=5*/s32[]{:T(128)}) while((s32[]{:T(128)}, f32[128,64]{0,1:T(8,128)S(1)}, pred[4,256,128]{2,1,0:T(8,128)(4,1)S(1)}, f32[4,256,64]{2,1,0:T(8,128)S(1)}, s32[]{:T(128)}, ...), condition=%wide.region_13.14_spmd.clone, body=%wide.region_11.13_spmd.clone.sunk | while | flops 4202499 | bytes 426071 | solution.py:98
  412.4 72.4 %pmax.43 = f32[8192]{0:T(1024)S(1)} all-reduce(f32[8192]{0:T(1024)S(1)} %reshape.213), channel_id=1, replica_groups=mesh['item'=16,'code'=8] {'item'}, use_global_device_ids=true, to_apply=%region_14.15 | all-reduce | flops 8192 | bytes 65536 | tf_op jit(solution)/shard_map/pmax | solution.py:115
  484.8 20.9 %all-gather = f32[131072]{0:T(1024)S(1)} all-gather(f32[8192]{0:T(1024)S(1)} %exponential_multiply_fusion.2), channel_id=2, replica_groups=mesh['item'=16,'code'=8] {'item'}, dimensions={0}, use_global_device_ids=true | all-gather | bytes 557056 | tf_op jit(solution)/shard_map/all_gather | solution.py:117
  509.5 11.8 %add_reduce_fusion.3 = f32[8,8,64]{2,1,0:T(8,128)S(1)} fusion(f32[8,8,16,64,64]{3,4,2,1,0:T(8,128)} %get-tuple-element.105, f32[8,8,16,64]{3,2,1,0:T(8,128)S(1)} %bitcast.97), kind=kLoop, calls=%fused_computation.35 | loop fusion | flops 8384512 | bytes 17055744 | tf_op jit(solution)/shard_map/reduce_max | solution.py:70
  521.3 11.9 %exponential_reduce_fusion.3 = f32[8,8,64]{2,1,0:T(8,128)S(1)} fusion(f32[8,8,16,64,64]{3,4,2,1,0:T(8,128)} %get-tuple-element.105, f32[8,8,64]{2,1,0:T(8,128)S(1)} %add_reduce_fusion.3, f32[8,8,16,64]{3,2,1,0:T(8,128)S(1)} %bitcast.98), kind=kLoop, calls=%fused_computation.29 | loop fusion | flops 12578816 | bytes 17072128 | tf_op jit(solution)/shard_map/reduce_sum | solution.py:71
  533.4 23.5 %pmax.44 = f32[4096]{0:T(1024)S(1)} all-reduce(f32[4096]{0:T(1024)S(1)} %reshape.219), channel_id=1, replica_groups=mesh['item'=16,'code'=8] {'code'}, use_global_device_ids=true, to_apply=%region_18.19 | all-reduce | flops 4096 | bytes 32768 | tf_op jit(solution)/shard_map/pmax | solution.py:77
  556.9 23.6 %psum.38 = f32[4096]{0:T(1024)S(1)} all-reduce(f32[4096]{0:T(1024)S(1)} %exponential_multiply_fusion.4), channel_id=1, replica_groups=mesh['item'=16,'code'=8] {'code'}, use_global_device_ids=true, to_apply=%region_20.21 | all-reduce | flops 4096 | bytes 32768 | tf_op jit(solution)/shard_map/psum | solution.py:78
  580.6 15.3 %add_reduce_fusion.2 = f32[8,8,16,64]{3,2,1,0:T(8,128)S(1)} fusion(f32[8,8,16,64,64]{3,4,2,1,0:T(8,128)} %get-tuple-element.105, f32[8,8,64]{2,1,0:T(8,128)S(1)} %add.157), kind=kLoop, calls=%fused_computation.34 | loop fusion | flops 8323072 | bytes 17055744 | tf_op jit(solution)/shard_map/reduce_max | solution.py:84
  595.9 20.7 %exponential_reduce_fusion.2 = f32[8,8,16,64]{3,2,1,0:T(8,128)S(1)} fusion(f32[8,8,16,64,64]{3,4,2,1,0:T(8,128)} %get-tuple-element.105, f32[8,8,16,64]{3,2,1,0:T(8,128)S(1)} %add_reduce_fusion.2, f32[8,8,64]{2,1,0:T(8,128)S(1)} %add.157), kind=kLoop, calls=%fused_computation.28 | loop fusion | flops 12517376 | bytes 17317888 | tf_op jit(solution)/shard_map/reduce_sum | solution.py:85
  616.6 13.3 %while.45 = (s32[]{:T(128)}, f32[128,64]{0,1:T(8,128)S(1)}, pred[4,256,128]{2,1,0:T(8,128)(4,1)S(1)}, f32[4,256,64]{2,1,0:T(8,128)S(1)}, s32[]{:T(128)}, /*index=5*/s32[]{:T(128)}) while((s32[]{:T(128)}, f32[128,64]{0,1:T(8,128)S(1)}, pred[4,256,128]{2,1,0:T(8,128)(4,1)S(1)}, f32[4,256,64]{2,1,0:T(8,128)S(1)}, s32[]{:T(128)}, ...), condition=%wide.region_24.25_spmd.clone, body=%wide.region_22.24_spmd.clone.sunk | while | flops 4202499 | bytes 426071 | solution.py:98
  633.8 72.1 %pmax.45 = f32[8192]{0:T(1024)S(1)} all-reduce(f32[8192]{0:T(1024)S(1)} %reshape.221), channel_id=1, replica_groups=mesh['item'=16,'code'=8] {'item'}, use_global_device_ids=true, to_apply=%region_25.26 | all-reduce | flops 8192 | bytes 65536 | tf_op jit(solution)/shard_map/pmax | solution.py:115
  705.9 20.9 %all-gather.1 = f32[131072]{0:T(1024)S(1)} all-gather(f32[8192]{0:T(1024)S(1)} %exponential_multiply_fusion.1), channel_id=3, replica_groups=mesh['item'=16,'code'=8] {'item'}, dimensions={0}, use_global_device_ids=true | all-gather | bytes 557056 | tf_op jit(solution)/shard_map/all_gather | solution.py:117
  730.0 11.8 %add_reduce_fusion.1 = f32[8,8,64]{2,1,0:T(8,128)S(1)} fusion(f32[8,8,16,64,64]{3,4,2,1,0:T(8,128)} %get-tuple-element.105, f32[8,8,16,64]{3,2,1,0:T(8,128)S(1)} %bitcast.95), kind=kLoop, calls=%fused_computation.33 | loop fusion | flops 8384512 | bytes 17055744 | tf_op jit(solution)/shard_map/reduce_max | solution.py:70
  741.8 11.9 %exponential_reduce_fusion.1 = f32[8,8,64]{2,1,0:T(8,128)S(1)} fusion(f32[8,8,16,64,64]{3,4,2,1,0:T(8,128)} %get-tuple-element.105, f32[8,8,64]{2,1,0:T(8,128)S(1)} %add_reduce_fusion.1, f32[8,8,16,64]{3,2,1,0:T(8,128)S(1)} %bitcast.96), kind=kLoop, calls=%fused_computation.27 | loop fusion | flops 12578816 | bytes 17072128 | tf_op jit(solution)/shard_map/reduce_sum | solution.py:71
  753.8 23.5 %pmax.46 = f32[4096]{0:T(1024)S(1)} all-reduce(f32[4096]{0:T(1024)S(1)} %reshape.226), channel_id=1, replica_groups=mesh['item'=16,'code'=8] {'code'}, use_global_device_ids=true, to_apply=%region_29.30 | all-reduce | flops 4096 | bytes 32768 | tf_op jit(solution)/shard_map/pmax | solution.py:77
  777.4 23.8 %psum.39 = f32[4096]{0:T(1024)S(1)} all-reduce(f32[4096]{0:T(1024)S(1)} %exponential_multiply_fusion.3), channel_id=1, replica_groups=mesh['item'=16,'code'=8] {'code'}, use_global_device_ids=true, to_apply=%region_31.32 | all-reduce | flops 4096 | bytes 32768 | tf_op jit(solution)/shard_map/psum | solution.py:78
  801.3 15.3 %add_reduce_fusion = f32[8,8,16,64]{3,2,1,0:T(8,128)S(1)} fusion(f32[8,8,16,64,64]{3,4,2,1,0:T(8,128)} %get-tuple-element.105, f32[8,8,64]{2,1,0:T(8,128)S(1)} %add.165), kind=kLoop, calls=%fused_computation.32 | loop fusion | flops 8323072 | bytes 17055744 | tf_op jit(solution)/shard_map/reduce_max | solution.py:84
  816.6 20.7 %exponential_reduce_fusion = f32[8,8,16,64]{3,2,1,0:T(8,128)S(1)} fusion(f32[8,8,16,64,64]{3,4,2,1,0:T(8,128)} %get-tuple-element.105, f32[8,8,16,64]{3,2,1,0:T(8,128)S(1)} %add_reduce_fusion, f32[8,8,64]{2,1,0:T(8,128)S(1)} %add.165), kind=kLoop, calls=%fused_computation.26 | loop fusion | flops 12517376 | bytes 17317888 | tf_op jit(solution)/shard_map/reduce_sum | solution.py:85
  837.3 13.3 %while.46 = (s32[]{:T(128)}, f32[128,64]{0,1:T(8,128)S(1)}, pred[4,256,128]{2,1,0:T(8,128)(4,1)S(1)}, f32[4,256,64]{2,1,0:T(8,128)S(1)}, s32[]{:T(128)}, /*index=5*/s32[]{:T(128)}) while((s32[]{:T(128)}, f32[128,64]{0,1:T(8,128)S(1)}, pred[4,256,128]{2,1,0:T(8,128)(4,1)S(1)}, f32[4,256,64]{2,1,0:T(8,128)S(1)}, s32[]{:T(128)}, ...), condition=%wide.region_35.36_spmd.clone, body=%wide.region_33.35_spmd.clone.sunk | while | flops 4202499 | bytes 426071 | solution.py:98
  854.5 72.1 %pmax.47 = f32[8192]{0:T(1024)S(1)} all-reduce(f32[8192]{0:T(1024)S(1)} %reshape.228), channel_id=1, replica_groups=mesh['item'=16,'code'=8] {'item'}, use_global_device_ids=true, to_apply=%region_36.37 | all-reduce | flops 8192 | bytes 65536 | tf_op jit(solution)/shard_map/pmax | solution.py:115
  926.6 20.9 %all-gather.2 = f32[131072]{0:T(1024)S(1)} all-gather(f32[8192]{0:T(1024)S(1)} %exponential_multiply_fusion), channel_id=4, replica_groups=mesh['item'=16,'code'=8] {'item'}, dimensions={0}, use_global_device_ids=true | all-gather | bytes 557056 | tf_op jit(solution)/shard_map/all_gather | solution.py:117
  (175 shorter events, 72.5 us)
Async XLA Ops:
  7.2 51.8 %all-gather.8.cloned.1.call-start = ((), (), s32[]{:S(2)}) async-start(), calls=%async_computation.1 | async-start | bytes 4718592 | tf_op jit(solution)/shard_map/all_gather | solution.py:14
  7.9 109.4 %all-gather.6.cloned.1.call-start = ((), (), s32[]{:S(2)}) async-start(), calls=%async_computation | async-start | bytes 8912896 | tf_op jit(solution)/shard_map/all_gather | solution.py:15
  285.0 74.0 %copy-start.3 = (f32[4096]{0:T(1024)S(1)}, f32[4096]{0:T(1024)}, u32[]{:S(2)}) copy-start(f32[4096]{0:T(1024)} %param.15) | copy-start | bytes 49156
  359.1 147.5 %copy-start.2 = (f32[8192]{0:T(1024)S(1)}, f32[8192]{0:T(1024)}, u32[]{:S(2)}) copy-start(f32[8192]{0:T(1024)} %param.16) | copy-start | bytes 98308
  580.6 36.0 %copy-start.1 = (f32[128,64]{0,1:T(8,128)S(1)}, f32[128,64]{0,1:T(8,128)}, u32[]{:S(2)}) copy-start(f32[128,64]{0,1:T(8,128)} %custom-call.1) | copy-start | bytes 98308
  801.2 36.1 %copy-start.4 = (f32[4096]{0:T(1024)}, f32[4096]{0:T(1024)S(1)}, u32[]{:S(2)}) copy-start(f32[4096]{0:T(1024)S(1)} %add_subtract_fusion.3) | copy-start | bytes 49156
  801.3 36.0 %copy-start = (f32[128,64]{0,1:T(8,128)S(1)}, f32[128,64]{0,1:T(8,128)}, u32[]{:S(2)}) copy-start(f32[128,64]{0,1:T(8,128)} %custom-call.2) | copy-start | bytes 98308
Sparse Core Ops, SparseCore 0:
  9.7 34.5 all-gather.7
  46.4 70.8 all-gather.5
